TPU v7x, 256 devices: a whole 4x4x8 slice. The times are simulated.
256 devices in a mesh: item: 64 (over z, y, x_lo), user: 4 (over x_hi, core).
Axes of the slice: x: 4 (x_hi: 2, x_lo: 2; x = x_hi * 2 + x_lo), y: 4, z: 8, core: 2. Of those that a mesh axis runs over, the one named last changes fastest.
Arguments:
- query_a: bfloat16 [4096, 256], P(('item', 'user')), may hold values from -8 to 8
- query_b: bfloat16 [4096, 256], P(('item', 'user')), may hold values from -8 to 8
- items: bfloat16 [131072, 256], P('item'), may hold values from -1 to 1
- positive_a: int32 [4096], replicated, may hold values from 0 to 131071
- positive_b: int32 [4096], replicated, may hold values from 0 to 131071
- loss_cotangent: float32 [4096], replicated, may hold values from -4 to 4
Outputs:
- loss_a: float32 [4096], P(('item', 'user'))
- grad_query_b: float32 [4096, 256], P(('item', 'user'))
- grad_items: float32 [131072, 256], P(('item', 'user'))
All inputs are finite; a program needn't handle non-finite values.
Results may differ from a plain program's by a relative error of at most 0.003.
Values may be sent and summed in bfloat16 or wider, within the bound.
A program may use at most 64 MiB of HBM per device.

v0:
```python
import functools

import jax
import jax.numpy as jnp
from jax import lax
from jax.experimental import pallas as pl
from jax.experimental.pallas import tpu as pltpu
from jax.sharding import PartitionSpec as P

MESH = pl.DeviceIdType.MESH
F32 = jnp.float32
BF16 = jnp.bfloat16
HIGHEST = lax.Precision.HIGHEST

NZ, NY, NX = 8, 4, 2
OWN = 16
E = 256
GROUP = NZ * NY * NX * OWN
HALF = GROUP // NX
TILE = 512
QUARTER = 512


def remote(src, dst, send_sem, recv_sem, device):
    return pltpu.make_async_remote_copy(
        src_ref=src,
        dst_ref=dst,
        send_sem=send_sem,
        recv_sem=recv_sem,
        device_id=device,
        device_id_type=MESH,
    )


def group_row(table, selector, row_of):
    picked = jnp.dot(table, selector, precision=HIGHEST, preferred_element_type=F32)
    rows = lax.broadcasted_iota(jnp.int32, picked.shape, 0)
    return jnp.sum(jnp.where(rows == row_of, picked, 0.0), axis=0, keepdims=True)


def lse_of(parts):
    top = jnp.max(parts, axis=0)
    return top + jnp.log(jnp.sum(jnp.exp(parts - top[None]), axis=0))


def kernel(
    qa_in, qb_in, items_in, pa_in, pb_in, w_in,
    loss_out, gq_out, gi_out,
    items_v, items_t, qa, qb, pa_v, pb_v, w_v, pos_a, pos_b, weight,
    probs, score_a, dsc, gq_f, gq_s,
    r1, gq_h, r2,
    gi_f, gi_s, gi_core, gi_far,
    zb, yb, za, ya,
    tops,
    in_sem, b1_s, b1_r, b2_s, b2_r, a1_s, a1_r, a2_s, a2_r,
    b_zs, b_zr, b_ys, b_yr, a_zs, a_zr, a_ys, a_yr,
    s1s, s1r, s2s, s2r, gi_ss, gi_rs, far_s, far_r,
):
    item = lax.axis_index("item")
    user = lax.axis_index("user")
    z, y, x = item // (NY * NX), (item // NX) % NY, item % NX
    place = y * NX + x
    far, core = user // 2, user % 2
    items_rows = items_v.shape[0]
    offset = item * items_rows

    def at(zz, yy, xx):
        return {"item": (zz * NY + yy) * NX + xx}

    def z_peer(k):
        return lax.rem(z + k, NZ)

    def y_peer(k):
        return lax.rem(y + k, NY)

    def plane_peer(k):
        return lax.rem(place + k, NY * NX)

    loads = [
        pltpu.make_async_copy(source, target, in_sem.at[n])
        for n, (source, target) in enumerate(
            (
                (qb_in, qb.at[x, y, z]),
                (qa_in, qa.at[x, y, z]),
                (pa_in, pa_v),
                (pb_in, pb_v),
                (w_in, w_v),
                (items_in, items_v),
            )
        )
    ]

    barrier = pltpu.get_barrier_semaphore()

    @pl.loop(1, NZ)
    def _(k):
        pl.semaphore_signal(barrier, inc=1, device_id=at(z_peer(k), y, x), device_id_type=MESH)
        pl.semaphore_signal(barrier, inc=1, device_id=at(z_peer(k), y, 1 - x), device_id_type=MESH)

    @pl.loop(1, NY * NX)
    def _(k):
        p = plane_peer(k)
        pl.semaphore_signal(barrier, inc=1, device_id=at(z, p // NX, p % NX), device_id_type=MESH)

    other_core = {"user": far * 2 + 1 - core}
    other_far = {"user": (1 - far) * 2 + core}
    pl.semaphore_signal(barrier, inc=1, device_id=other_core, device_id_type=MESH)
    pl.semaphore_signal(barrier, inc=1, device_id=other_far, device_id_type=MESH)

    for load in loads:
        load.start()

    pl.semaphore_wait(barrier, 2 * (NZ - 1) + (NY * NX - 1) + 2)

    def sent(refs, send_sem, recv_sem):
        remote(refs, refs, send_sem, recv_sem, other_core).wait_send()

    def arrived(refs, send_sem, recv_sem):
        remote(refs, refs, send_sem, recv_sem, other_core).wait_recv()

    @pl.loop(1, NZ)
    def _(k):
        remote(qb_in, qb.at[x, y, z], b1_s, b1_r, at(z_peer(k), y, x)).start()

    def gather_b_bulk():
        block = qb.at[x, y]

        @pl.loop(1, NY)
        def _(k):
            remote(block, block, b2_s, b2_r.at[x], at(z, y_peer(k), x)).start()

        @pl.loop(0, NY)
        def _(k):
            remote(block, block, b2_s, b2_r.at[x], at(z, y_peer(k), 1 - x)).start()

    @pl.loop(1, NY * NX)
    def _(k):
        p = plane_peer(k)
        remote(qa_in, qa.at[x, y, z], a1_s, a1_r, at(z, p // NX, p % NX)).start()

    def gather_a_bulk(xx):
        block = qa.at[xx, :, z]

        @pl.loop(1, NZ)
        def _(k):
            remote(block, block, a2_s, a2_r.at[xx], at(z_peer(k), y, x)).start()

    others = pl.ds(0, NZ - 1)

    lanes = lax.broadcasted_iota(jnp.int32, (1, GROUP), 1)
    own_of = lanes % OWN
    z_of = (lanes // OWN) % NZ
    y_of = (lanes // (OWN * NZ)) % NY
    x_of = lanes // (OWN * NZ * NY)
    ks = lax.broadcasted_iota(jnp.int32, (128, GROUP), 0)
    selector = (ks == x_of * (4 * OWN) + user * OWN + own_of).astype(F32)
    row_of = z_of * NY + y_of
    for load in loads[2:5]:
        load.wait()
    pos_a[...] = group_row(pa_v[...].astype(F32), selector, row_of).astype(jnp.int32) - offset
    pos_b[...] = group_row(pb_v[...].astype(F32), selector, row_of).astype(jnp.int32) - offset
    weight[...] = group_row(w_v[...], selector, row_of)

    loads[0].wait()
    arrived(qb.at[x, y, others], b1_s, b1_r)
    gather_b_bulk()
    loads[1].wait()
    arrived(qa.at[x, y, others], a1_s, a1_r)
    gather_a_bulk(x)

    loads[5].wait()
    for part in range(items_rows // QUARTER):
        rows = pl.ds(part * QUARTER, QUARTER)
        items_t[:, rows] = items_v[rows, :].T

    tiles = items_rows // TILE

    def half_of(xx):
        return pl.ds(pl.multiple_of(xx * HALF, HALF), HALF)

    def tile_of(t):
        return pl.ds(pl.multiple_of(t * TILE, TILE), TILE)

    def fold(values, op):
        return op(values.reshape(TILE // 8, 8, HALF), axis=0)

    def scores(q, xx):
        users = q[xx].reshape(HALF, E)
        return lax.dot_general(
            items_v[...], users, (((1,), (1,)), ((), ())), preferred_element_type=F32
        )

    zero = jnp.zeros((8, HALF), F32)
    least = jnp.full((8, HALF), -jnp.inf, F32)

    def half_b(xx):
        probs[xx] = scores(qb, xx)

        def largest(t, top):
            return jnp.maximum(top, fold(probs[xx, tile_of(t), :], jnp.max))

        top = jnp.max(lax.fori_loop(0, tiles, largest, least), axis=0, keepdims=True)

        def exponentials(t, total):
            p = jnp.exp(probs[xx, tile_of(t), :] - top)
            probs[xx, tile_of(t), :] = p
            return total + fold(p, jnp.sum)

        total = jnp.sum(lax.fori_loop(0, tiles, exponentials, zero), axis=0, keepdims=True)
        tops[:, half_of(xx)] = top
        zb[z, :, half_of(xx)] = top + jnp.log(total)

    def half_a(xx):
        score_a[...] = scores(qa, xx)
        pos = pos_a[:, half_of(xx)]
        ids = lax.broadcasted_iota(jnp.int32, (TILE, HALF), 0)

        def largest(t, carry):
            top, hit = carry
            score = score_a[tile_of(t), :]
            match = jnp.where(ids == pos - t * TILE, score, 0.0)
            return jnp.maximum(top, fold(score, jnp.max)), hit + fold(match, jnp.sum)

        top, hit = lax.fori_loop(0, tiles, largest, (least, zero))
        top = jnp.max(top, axis=0, keepdims=True)

        def exponentials(t, total):
            return total + fold(jnp.exp(score_a[tile_of(t), :] - top), jnp.sum)

        total = jnp.sum(lax.fori_loop(0, tiles, exponentials, zero), axis=0, keepdims=True)
        za[z, 0:1, half_of(xx)] = top + jnp.log(total)
        za[z, 1:2, half_of(xx)] = jnp.sum(hit, axis=0, keepdims=True)

    def z_round(buf, ss, rs):
        @pl.loop(1, NZ)
        def _(k):
            remote(buf.at[z], buf.at[z], ss, rs, at(z_peer(k), y, x)).start()

    def plane_round(buf, ss, rs):
        @pl.loop(1, NY * NX)
        def _(k):
            p = plane_peer(k)
            remote(buf.at[place], buf.at[place], ss, rs, at(z, p // NX, p % NX)).start()

    arrived(qb.at[x, pl.ds(0, NY - 1)], b2_s, b2_r.at[x])
    half_b(x)
    arrived(qb.at[1 - x], b2_s, b2_r.at[1 - x])
    half_b(1 - x)
    z_round(zb, b_zs, b_zr)
    gather_a_bulk(1 - x)
    sent(qb.at[x, y, others], b1_s, b1_r)
    sent(qa.at[x, y, others], a1_s, a1_r)
    sent(qb.at[0], b2_s, b2_r.at[0])
    sent(qb.at[0, pl.ds(0, NY - 1)], b2_s, b2_r.at[0])
    arrived(zb.at[others], b_zs, b_zr)
    yb[place] = lse_of(zb[...])
    plane_round(yb, b_ys, b_yr)
    arrived(qa.at[x, :, others], a2_s, a2_r.at[x])
    half_a(x)
    sent(zb.at[others], b_zs, b_zr)

    arrived(yb.at[others], b_ys, b_yr)
    factor = weight[...] * jnp.exp(tops[...] - lse_of(yb[...]))

    ids = lax.broadcasted_iota(jnp.int32, (TILE, HALF), 0)

    def quarter_of(ff, cc):
        return pl.ds(pl.multiple_of((ff * 2 + cc) * QUARTER, QUARTER), QUARTER)

    def dscores(ff, cc):
        rows = quarter_of(ff, cc)
        for xx in range(NX):
            cols = slice(xx * HALF, (xx + 1) * HALF)
            match = jnp.where(
                ids == pos_b[:, cols] - (ff * 2 + cc) * QUARTER, weight[:, cols], 0.0
            )
            dsc[rows, cols] = (probs[xx, rows, :] * factor[:, cols] - match).astype(BF16)

    def far_copy():
        return remote(gi_s, gi_far, far_s, far_r, other_far)

    def core_copy(n):
        return remote(gi_f.at[n, 1 - core], gi_core.at[n], gi_ss.at[n], gi_rs.at[n], other_core)

    def item_grads(n, ff, cc):
        gi_f[n, cc] = jnp.dot(
            dsc[quarter_of(ff, cc), :], qb[...].reshape(GROUP, E), preferred_element_type=F32
        )

    def query_grads(xx):
        block = jnp.dot(
            items_t[...], dsc[:, half_of(xx)], preferred_element_type=F32
        ).T.reshape(NY, NZ, OWN, E)
        gq_f[xx] = block
        gq_s[xx] = block.astype(BF16)

        @pl.loop(1, NY)
        def _(k):
            yy = y_peer(k)
            remote(gq_s.at[xx, yy], r1.at[place], s1s, s1r, at(z, yy, xx)).start()

        @pl.when(x != xx)
        def _():
            remote(gq_s.at[xx, y], r1.at[place], s1s, s1r, at(z, y, xx)).start()

    dscores(1 - far, 1 - core)
    item_grads(0, 1 - far, 1 - core)
    core_copy(0).start()
    dscores(1 - far, core)
    item_grads(0, 1 - far, core)
    dscores(far, 1 - core)
    dscores(far, core)
    query_grads(1 - x)
    core_copy(0).wait_recv()
    gi_s[...] = (gi_f[0, core] + gi_core[0]).astype(BF16)
    far_copy().start()

    query_grads(x)
    item_grads(1, far, 1 - core)
    core_copy(1).start()
    item_grads(1, far, core)

    arrived(qa.at[1 - x, :, others], a2_s, a2_r.at[1 - x])
    half_a(1 - x)
    z_round(za, a_zs, a_zr)

    r1[place] = jnp.zeros((NZ, OWN, E), BF16)
    r2[z] = jnp.zeros((OWN, E), F32)
    arrived(r1.at[others], s1s, s1r)
    gq_h[...] = gq_f[x, y] + jnp.sum(r1[...].astype(F32), axis=0)

    @pl.loop(1, NZ)
    def _(k):
        zz = z_peer(k)
        remote(gq_h.at[zz], r2.at[z], s2s, s2r, at(zz, y, x)).start()

    arrived(za.at[others], a_zs, a_zr)
    z_parts = za[...]
    ya[place, 0:1] = lse_of(z_parts[:, 0:1])
    ya[place, 1:2] = jnp.sum(z_parts[:, 1:2], axis=0)
    plane_round(ya, a_ys, a_yr)

    core_copy(1).wait_recv()
    gi_out[...] = gi_f[1, core] + gi_core[1]
    sent(qa.at[0, :, others], a2_s, a2_r.at[0])
    sent(qa.at[1, :, others], a2_s, a2_r.at[0])
    sent(yb.at[others], b_ys, b_yr)
    sent(za.at[others], a_zs, a_zr)
    sent(r1.at[others], s1s, s1r)
    core_copy(0).wait_send()
    core_copy(1).wait_send()
    far_copy().wait_recv()
    gi_out[...] += gi_far[...].astype(F32)

    arrived(ya.at[others], a_ys, a_yr)
    y_parts = ya[...]
    tops[...] = lse_of(y_parts[:, 0:1]) - jnp.sum(y_parts[:, 1:2], axis=0)
    mine = tops[:, pl.ds(pl.multiple_of((x * NY + y) * NZ * OWN, NZ * OWN), NZ * OWN)]
    pick_row = lax.broadcasted_iota(jnp.int32, (NZ * OWN, OWN), 0)
    pick_col = lax.broadcasted_iota(jnp.int32, (NZ * OWN, OWN), 1)
    pick = (pick_row == z * OWN + pick_col).astype(F32)
    loss_out[...] = jnp.dot(mine, pick, precision=HIGHEST, preferred_element_type=F32)

    arrived(r2.at[others], s2s, s2r)
    gq_out[...] = gq_h[z] + jnp.sum(r2[...], axis=0)

    sent(ya.at[others], a_ys, a_yr)
    sent(r2.at[others], s2s, s2r)

    far_copy().wait_send()


def hand_over(*refs):
    copies = [
        pltpu.make_async_copy(source, target, refs[6].at[n])
        for n, (source, target) in enumerate(zip(refs[:3], refs[3:6]))
    ]
    for copy in copies:
        copy.start()
    for copy in copies:
        copy.wait()


def per_device(query_a, query_b, items, positive_a, positive_b, loss_cotangent):
    rows = items.shape[0]
    hbm, vmem = pl.BlockSpec(memory_space=pltpu.HBM), pl.BlockSpec(memory_space=pltpu.VMEM)
    results = (
        jax.ShapeDtypeStruct((1, OWN), F32),
        jax.ShapeDtypeStruct((OWN, E), F32),
        jax.ShapeDtypeStruct((QUARTER, E), F32),
    )
    dma = pltpu.SemaphoreType.DMA
    block = (NX, NY, NZ, OWN, E)
    loss, gq, gi = pl.pallas_call(
        kernel,
        out_shape=[pltpu.VMEM(r.shape, r.dtype) for r in results],
        in_specs=[hbm] * 6,
        out_specs=[vmem] * 3,
        scratch_shapes=[
            pltpu.VMEM((rows, E), BF16),
            pltpu.VMEM((E, rows), BF16),
            pltpu.VMEM(block, BF16),
            pltpu.VMEM(block, BF16),
            pltpu.VMEM((32, 128), jnp.int32),
            pltpu.VMEM((32, 128), jnp.int32),
            pltpu.VMEM((32, 128), F32),
            pltpu.VMEM((1, GROUP), jnp.int32),
            pltpu.VMEM((1, GROUP), jnp.int32),
            pltpu.VMEM((1, GROUP), F32),
            pltpu.VMEM((NX, rows, HALF), F32),
            pltpu.VMEM((rows, HALF), F32),
            pltpu.VMEM((rows, GROUP), BF16),
            pltpu.VMEM(block, F32),
            pltpu.VMEM(block, BF16),
            pltpu.VMEM((NY * NX, NZ, OWN, E), BF16),
            pltpu.VMEM((NZ, OWN, E), F32),
            pltpu.VMEM((NZ, OWN, E), F32),
            pltpu.VMEM((2, 2, QUARTER, E), F32),
            pltpu.VMEM((QUARTER, E), BF16),
            pltpu.VMEM((2, QUARTER, E), F32),
            pltpu.VMEM((QUARTER, E), BF16),
            pltpu.VMEM((NZ, 1, GROUP), F32),
            pltpu.VMEM((NY * NX, 1, GROUP), F32),
            pltpu.VMEM((NZ, 2, GROUP), F32),
            pltpu.VMEM((NY * NX, 2, GROUP), F32),
            pltpu.VMEM((1, GROUP), F32),
            dma((6,)),
            dma, dma,
            dma, dma((NX,)),
            dma, dma,
            dma, dma((NX,)),
            dma, dma,
            dma, dma,
            dma, dma,
            dma, dma,
            dma, dma,
            dma, dma,
            dma((2,)), dma((2,)),
            dma, dma,
        ],
        compiler_params=pltpu.CompilerParams(
            collective_id=0, has_side_effects=True, vmem_limit_bytes=56 * 1024 * 1024
        ),
    )(
        *(
            pltpu.with_memory_space_constraint(operand, pltpu.HBM)
            for operand in (
                query_a,
                query_b,
                items,
                positive_a.reshape(32, 128),
                positive_b.reshape(32, 128),
                loss_cotangent.reshape(32, 128),
            )
        )
    )
    loss, gq, gi = pl.pallas_call(
        hand_over,
        out_shape=results,
        in_specs=[vmem] * 3,
        out_specs=[hbm] * 3,
        scratch_shapes=[dma((3,))],
        compiler_params=pltpu.CompilerParams(vmem_limit_bytes=1024 * 1024),
    )(*(pltpu.with_memory_space_constraint(result, pltpu.VMEM) for result in (loss, gq, gi)))
    return loss.reshape(OWN), gq, gi


def solution(mesh):
    return jax.shard_map(
        per_device,
        mesh=mesh,
        in_specs=(
            P(("item", "user"), None),
            P(("item", "user"), None),
            P("item", None),
            P(),
            P(),
            P(),
        ),
        out_specs=(P(("item", "user")), P(("item", "user"), None), P(("item", "user"), None)),
        check_vma=False,
    )
```

profile of v0, /device:TPU:2, one launch (start us, length us, event | category | flops | bytes accessed | tf_op | source)
XLA Modules:
  0.0 52.6 jit_solution(12498095631407212716)
XLA Ops:
  0.6 51.1 %shard_map.85 = (f32[1,16]{1,0:T(1,128)S(1)}, f32[16,256]{1,0:T(8,128)S(1)}, f32[512,256]{1,0:T(8,128)S(1)}) custom-call(bf16[16,256]{1,0:T(8,128)(2,1)} %qa_in.1, bf16[16,256]{1,0:T(8,128)(2,1)} %qb_in.1, bf16[2048,256]{1,0:T(8,128)(2,1)} %items_in.1, s32[32,128]{1,0:T(8,128)} %bitcast.4, s32[32,128]{1,0:T(8,128)} %bitcast.5, f32[32,128]{1,0:T(8,128)} %bitcast.6), custom_call_target="tpu_custom_call" | custom-call | tf_op jit(solution)/shard_map/pallas_call | solution.py:394
  51.7 0.8 %shard_map.86 = (f32[1,16]{1,0:T(1,128)}, f32[16,256]{1,0:T(8,128)}, f32[512,256]{1,0:T(8,128)}) custom-call(f32[1,16]{1,0:T(1,128)S(1)} %get-tuple-element.9.refs_0_, f32[16,256]{1,0:T(8,128)S(1)} %get-tuple-element.10.refs_1_, f32[512,256]{1,0:T(8,128)S(1)} %get-tuple-element.11.refs_2_), custom_call_target="tpu_custom_call" | custom-call | tf_op jit(solution)/shard_map/pallas_call | solution.py:457
where the time goes:
time: 53.2 us; the launch traced here: 52.6 us
  Pallas kernels  51.9 us (98%)
  between operations  0.64 us (1%)
    pallas_call x1, Pallas kernels, per_device(): pl.pallas_call(kernel, out_shape=[pltpu.VMEM(r.shape, r.dtype) for r in r...  51.1 us

commit v1 on v0

--- a/solution.py
+++ b/solution.py
@@ -51,7 +51,7 @@
     r1, gq_h, r2,
     gi_f, gi_s, gi_core, gi_far,
     zb, yb, za, ya,
-    tops,
+    tops, top_a,
     in_sem, b1_s, b1_r, b2_s, b2_r, a1_s, a1_r, a2_s, a2_r,
     b_zs, b_zr, b_ys, b_yr, a_zs, a_zr, a_ys, a_yr,
     s1s, s1r, s2s, s2r, gi_ss, gi_rs, far_s, far_r,
@@ -192,6 +192,7 @@
 
     zero = jnp.zeros((8, HALF), F32)
     least = jnp.full((8, HALF), -jnp.inf, F32)
+    ids = lax.broadcasted_iota(jnp.int32, (TILE, HALF), 0)
 
     def half_b(xx):
         probs[xx] = scores(qb, xx)
@@ -208,12 +209,13 @@
 
         total = jnp.sum(lax.fori_loop(0, tiles, exponentials, zero), axis=0, keepdims=True)
         tops[:, half_of(xx)] = top
-        zb[z, :, half_of(xx)] = top + jnp.log(total)
-
-    def half_a(xx):
+        zb[xx, z] = top + jnp.log(total)
+
+    def scores_a(xx):
         score_a[...] = scores(qa, xx)
+
+    def tops_a(xx):
         pos = pos_a[:, half_of(xx)]
-        ids = lax.broadcasted_iota(jnp.int32, (TILE, HALF), 0)
 
         def largest(t, carry):
             top, hit = carry
@@ -222,14 +224,17 @@
             return jnp.maximum(top, fold(score, jnp.max)), hit + fold(match, jnp.sum)
 
         top, hit = lax.fori_loop(0, tiles, largest, (least, zero))
-        top = jnp.max(top, axis=0, keepdims=True)
+        top_a[...] = jnp.max(top, axis=0, keepdims=True)
+        za[z, 1:2, half_of(xx)] = jnp.sum(hit, axis=0, keepdims=True)
+
+    def sums_a(xx):
+        top = top_a[...]
 
         def exponentials(t, total):
             return total + fold(jnp.exp(score_a[tile_of(t), :] - top), jnp.sum)
 
         total = jnp.sum(lax.fori_loop(0, tiles, exponentials, zero), axis=0, keepdims=True)
         za[z, 0:1, half_of(xx)] = top + jnp.log(total)
-        za[z, 1:2, half_of(xx)] = jnp.sum(hit, axis=0, keepdims=True)
 
     def z_round(buf, ss, rs):
         @pl.loop(1, NZ)
@@ -242,39 +247,42 @@
             p = plane_peer(k)
             remote(buf.at[place], buf.at[place], ss, rs, at(z, p // NX, p % NX)).start()
 
+    def lse_z(xx):
+        z_round(zb.at[xx], b_zs.at[xx], b_zr.at[xx])
+
+    def lse_plane(xx):
+        arrived(zb.at[xx, others], b_zs.at[xx], b_zr.at[xx])
+        yb[xx, place] = lse_of(zb[xx])
+        plane_round(yb.at[xx], b_ys.at[xx], b_yr.at[xx])
+
+    def dscores(xx):
+        arrived(yb.at[xx, others], b_ys.at[xx], b_yr.at[xx])
+        cols = half_of(xx)
+        pos, scale = pos_b[:, cols], weight[:, cols]
+        factor = scale * jnp.exp(tops[:, cols] - lse_of(yb[xx]))
+
+        @pl.loop(0, tiles)
+        def _(t):
+            match = jnp.where(ids == pos - t * TILE, scale, 0.0)
+            dsc[tile_of(t), cols] = (probs[xx, tile_of(t), :] * factor - match).astype(BF16)
+
     arrived(qb.at[x, pl.ds(0, NY - 1)], b2_s, b2_r.at[x])
     half_b(x)
+    lse_z(x)
     arrived(qb.at[1 - x], b2_s, b2_r.at[1 - x])
     half_b(1 - x)
-    z_round(zb, b_zs, b_zr)
+    lse_z(1 - x)
     gather_a_bulk(1 - x)
     sent(qb.at[x, y, others], b1_s, b1_r)
     sent(qa.at[x, y, others], a1_s, a1_r)
     sent(qb.at[0], b2_s, b2_r.at[0])
     sent(qb.at[0, pl.ds(0, NY - 1)], b2_s, b2_r.at[0])
-    arrived(zb.at[others], b_zs, b_zr)
-    yb[place] = lse_of(zb[...])
-    plane_round(yb, b_ys, b_yr)
     arrived(qa.at[x, :, others], a2_s, a2_r.at[x])
-    half_a(x)
-    sent(zb.at[others], b_zs, b_zr)
-
-    arrived(yb.at[others], b_ys, b_yr)
-    factor = weight[...] * jnp.exp(tops[...] - lse_of(yb[...]))
-
-    ids = lax.broadcasted_iota(jnp.int32, (TILE, HALF), 0)
-
-    def quarter_of(ff, cc):
-        return pl.ds(pl.multiple_of((ff * 2 + cc) * QUARTER, QUARTER), QUARTER)
-
-    def dscores(ff, cc):
-        rows = quarter_of(ff, cc)
-        for xx in range(NX):
-            cols = slice(xx * HALF, (xx + 1) * HALF)
-            match = jnp.where(
-                ids == pos_b[:, cols] - (ff * 2 + cc) * QUARTER, weight[:, cols], 0.0
-            )
-            dsc[rows, cols] = (probs[xx, rows, :] * factor[:, cols] - match).astype(BF16)
+    scores_a(x)
+    lse_plane(x)
+    tops_a(x)
+    lse_plane(1 - x)
+    sums_a(x)
 
     def far_copy():
         return remote(gi_s, gi_far, far_s, far_r, other_far)
@@ -283,8 +291,9 @@
         return remote(gi_f.at[n, 1 - core], gi_core.at[n], gi_ss.at[n], gi_rs.at[n], other_core)
 
     def item_grads(n, ff, cc):
+        rows = pl.ds(pl.multiple_of((ff * 2 + cc) * QUARTER, QUARTER), QUARTER)
         gi_f[n, cc] = jnp.dot(
-            dsc[quarter_of(ff, cc), :], qb[...].reshape(GROUP, E), preferred_element_type=F32
+            dsc[rows, :], qb[...].reshape(GROUP, E), preferred_element_type=F32
         )
 
     def query_grads(xx):
@@ -297,42 +306,41 @@
         @pl.loop(1, NY)
         def _(k):
             yy = y_peer(k)
-            remote(gq_s.at[xx, yy], r1.at[place], s1s, s1r, at(z, yy, xx)).start()
-
-        @pl.when(x != xx)
-        def _():
-            remote(gq_s.at[xx, y], r1.at[place], s1s, s1r, at(z, y, xx)).start()
-
-    dscores(1 - far, 1 - core)
+            remote(gq_s.at[xx, yy], r1.at[xx, y], s1s, s1r.at[xx], at(z, yy, x)).start()
+
+    def second_stage(xx):
+        r1[xx, y] = jnp.zeros((NZ, OWN, E), BF16)
+        arrived(r1.at[xx, pl.ds(0, NY - 1)], s1s, s1r.at[xx])
+        gq_h[xx] = gq_f[xx, y] + jnp.sum(r1[xx].astype(F32), axis=0)
+
+        @pl.loop(1, NZ)
+        def _(k):
+            zz = z_peer(k)
+            remote(gq_h.at[xx, zz], r2.at[x, z], s2s, s2r.at[x], at(zz, y, xx)).start()
+
+    dscores(x)
+    query_grads(x)
+    dscores(1 - x)
     item_grads(0, 1 - far, 1 - core)
     core_copy(0).start()
-    dscores(1 - far, core)
+    query_grads(1 - x)
     item_grads(0, 1 - far, core)
-    dscores(far, 1 - core)
-    dscores(far, core)
-    query_grads(1 - x)
     core_copy(0).wait_recv()
     gi_s[...] = (gi_f[0, core] + gi_core[0]).astype(BF16)
     far_copy().start()
-
-    query_grads(x)
     item_grads(1, far, 1 - core)
     core_copy(1).start()
+    second_stage(x)
     item_grads(1, far, core)
 
     arrived(qa.at[1 - x, :, others], a2_s, a2_r.at[1 - x])
-    half_a(1 - x)
+    scores_a(1 - x)
+    tops_a(1 - x)
+    sums_a(1 - x)
     z_round(za, a_zs, a_zr)
 
-    r1[place] = jnp.zeros((NZ, OWN, E), BF16)
-    r2[z] = jnp.zeros((OWN, E), F32)
-    arrived(r1.at[others], s1s, s1r)
-    gq_h[...] = gq_f[x, y] + jnp.sum(r1[...].astype(F32), axis=0)
-
-    @pl.loop(1, NZ)
-    def _(k):
-        zz = z_peer(k)
-        remote(gq_h.at[zz], r2.at[z], s2s, s2r, at(zz, y, x)).start()
+    second_stage(1 - x)
+    remote(gq_h.at[1 - x, z], r2.at[x, z], s2s, s2r.at[x], at(z, y, 1 - x)).start()
 
     arrived(za.at[others], a_zs, a_zr)
     z_parts = za[...]
@@ -344,9 +352,12 @@
     gi_out[...] = gi_f[1, core] + gi_core[1]
     sent(qa.at[0, :, others], a2_s, a2_r.at[0])
     sent(qa.at[1, :, others], a2_s, a2_r.at[0])
-    sent(yb.at[others], b_ys, b_yr)
+    for half in range(NX):
+        sent(zb.at[half, others], b_zs.at[half], b_zr.at[half])
+        sent(yb.at[half, others], b_ys.at[half], b_yr.at[half])
     sent(za.at[others], a_zs, a_zr)
-    sent(r1.at[others], s1s, s1r)
+    for half in range(NX):
+        sent(r1.at[half, pl.ds(0, NY - 1)], s1s, s1r.at[half])
     core_copy(0).wait_send()
     core_copy(1).wait_send()
     far_copy().wait_recv()
@@ -361,11 +372,14 @@
     pick = (pick_row == z * OWN + pick_col).astype(F32)
     loss_out[...] = jnp.dot(mine, pick, precision=HIGHEST, preferred_element_type=F32)
 
-    arrived(r2.at[others], s2s, s2r)
-    gq_out[...] = gq_h[z] + jnp.sum(r2[...], axis=0)
+    r2[x, z] = jnp.zeros((OWN, E), F32)
+    arrived(r2.at[x, others], s2s, s2r.at[x])
+    arrived(r2.at[1 - x], s2s, s2r.at[1 - x])
+    gq_out[...] = gq_h[x, z] + jnp.sum(r2[...].reshape(NX * NZ, OWN, E), axis=0)
 
     sent(ya.at[others], a_ys, a_yr)
-    sent(r2.at[others], s2s, s2r)
+    sent(r2.at[0], s2s, s2r.at[0])
+    sent(r2.at[1, others], s2s, s2r.at[1])
 
     far_copy().wait_send()
 
@@ -412,29 +426,30 @@
             pltpu.VMEM((rows, GROUP), BF16),
             pltpu.VMEM(block, F32),
             pltpu.VMEM(block, BF16),
-            pltpu.VMEM((NY * NX, NZ, OWN, E), BF16),
-            pltpu.VMEM((NZ, OWN, E), F32),
-            pltpu.VMEM((NZ, OWN, E), F32),
+            pltpu.VMEM(block, BF16),
+            pltpu.VMEM((NX, NZ, OWN, E), F32),
+            pltpu.VMEM((NX, NZ, OWN, E), F32),
             pltpu.VMEM((2, 2, QUARTER, E), F32),
             pltpu.VMEM((QUARTER, E), BF16),
             pltpu.VMEM((2, QUARTER, E), F32),
             pltpu.VMEM((QUARTER, E), BF16),
-            pltpu.VMEM((NZ, 1, GROUP), F32),
-            pltpu.VMEM((NY * NX, 1, GROUP), F32),
+            pltpu.VMEM((NX, NZ, 1, HALF), F32),
+            pltpu.VMEM((NX, NY * NX, 1, HALF), F32),
             pltpu.VMEM((NZ, 2, GROUP), F32),
             pltpu.VMEM((NY * NX, 2, GROUP), F32),
             pltpu.VMEM((1, GROUP), F32),
+            pltpu.VMEM((1, HALF), F32),
             dma((6,)),
             dma, dma,
             dma, dma((NX,)),
             dma, dma,
             dma, dma((NX,)),
+            dma((NX,)), dma((NX,)),
+            dma((NX,)), dma((NX,)),
             dma, dma,
             dma, dma,
-            dma, dma,
-            dma, dma,
-            dma, dma,
-            dma, dma,
+            dma, dma((NX,)),
+            dma, dma((NX,)),
             dma((2,)), dma((2,)),
             dma, dma,
         ],

time: 53.2 us -> 54.1 us (1.017)
  Pallas kernels: 51.9 us -> 52.6 us
    pallas_call x1, Pallas kernels: 51.1 us -> 51.7 us  [per_device(): pl.pallas_call(kernel, out_shape=[pltpu.VMEM(r.shape, r.dtype) for r in r...]
where the time goes in v1:
time: 54.1 us; the launch traced here: 53.2 us
  Pallas kernels  52.6 us (97%)
  between operations  0.64 us (1%)
    pallas_call x1, Pallas kernels, per_device(): pl.pallas_call(kernel, out_shape=[pltpu.VMEM(r.shape, r.dtype) for r in r...  51.7 us

profile of v1, /device:TPU:2, one launch (start us, length us, event | category | flops | bytes accessed | tf_op | source)
XLA Modules:
  0.0 53.2 jit_solution(12092764086993304649)
XLA Ops:
  0.6 51.7 %shard_map.85 = (f32[1,16]{1,0:T(1,128)S(1)}, f32[16,256]{1,0:T(8,128)S(1)}, f32[512,256]{1,0:T(8,128)S(1)}) custom-call(bf16[16,256]{1,0:T(8,128)(2,1)} %qa_in.1, bf16[16,256]{1,0:T(8,128)(2,1)} %qb_in.1, bf16[2048,256]{1,0:T(8,128)(2,1)} %items_in.1, s32[32,128]{1,0:T(8,128)} %bitcast.4, s32[32,128]{1,0:T(8,128)} %bitcast.5, f32[32,128]{1,0:T(8,128)} %bitcast.6), custom_call_target="tpu_custom_call" | custom-call | tf_op jit(solution)/shard_map/pallas_call | solution.py:408
  52.4 0.8 %shard_map.86 = (f32[1,16]{1,0:T(1,128)}, f32[16,256]{1,0:T(8,128)}, f32[512,256]{1,0:T(8,128)}) custom-call(f32[1,16]{1,0:T(1,128)S(1)} %get-tuple-element.9.refs_0_, f32[16,256]{1,0:T(8,128)S(1)} %get-tuple-element.10.refs_1_, f32[512,256]{1,0:T(8,128)S(1)} %get-tuple-element.11.refs_2_), custom_call_target="tpu_custom_call" | custom-call | tf_op jit(solution)/shard_map/pallas_call | solution.py:472

commit v2 on v0

--- a/solution.py
+++ b/solution.py
@@ -17,7 +17,7 @@
 E = 256
 GROUP = NZ * NY * NX * OWN
 HALF = GROUP // NX
-TILE = 512
+TILE = 32
 QUARTER = 512
 
 
@@ -173,13 +173,11 @@
         rows = pl.ds(part * QUARTER, QUARTER)
         items_t[:, rows] = items_v[rows, :].T
 
-    tiles = items_rows // TILE
+    tiles = [slice(r, r + TILE) for r in range(0, items_rows, TILE)]
+    ids = lax.broadcasted_iota(jnp.int32, (TILE, HALF), 0)
 
     def half_of(xx):
         return pl.ds(pl.multiple_of(xx * HALF, HALF), HALF)
-
-    def tile_of(t):
-        return pl.ds(pl.multiple_of(t * TILE, TILE), TILE)
 
     def fold(values, op):
         return op(values.reshape(TILE // 8, 8, HALF), axis=0)
@@ -196,38 +194,32 @@
     def half_b(xx):
         probs[xx] = scores(qb, xx)
 
-        def largest(t, top):
-            return jnp.maximum(top, fold(probs[xx, tile_of(t), :], jnp.max))
-
-        top = jnp.max(lax.fori_loop(0, tiles, largest, least), axis=0, keepdims=True)
-
-        def exponentials(t, total):
-            p = jnp.exp(probs[xx, tile_of(t), :] - top)
-            probs[xx, tile_of(t), :] = p
-            return total + fold(p, jnp.sum)
-
-        total = jnp.sum(lax.fori_loop(0, tiles, exponentials, zero), axis=0, keepdims=True)
+        top = least
+        for rows in tiles:
+            top = jnp.maximum(top, fold(probs[xx, rows, :], jnp.max))
+        top = jnp.max(top, axis=0, keepdims=True)
+        total = zero
+        for rows in tiles:
+            p = jnp.exp(probs[xx, rows, :] - top)
+            probs[xx, rows, :] = p
+            total = total + fold(p, jnp.sum)
+        total = jnp.sum(total, axis=0, keepdims=True)
         tops[:, half_of(xx)] = top
         zb[z, :, half_of(xx)] = top + jnp.log(total)
 
     def half_a(xx):
         score_a[...] = scores(qa, xx)
         pos = pos_a[:, half_of(xx)]
-        ids = lax.broadcasted_iota(jnp.int32, (TILE, HALF), 0)
-
-        def largest(t, carry):
-            top, hit = carry
-            score = score_a[tile_of(t), :]
-            match = jnp.where(ids == pos - t * TILE, score, 0.0)
-            return jnp.maximum(top, fold(score, jnp.max)), hit + fold(match, jnp.sum)
-
-        top, hit = lax.fori_loop(0, tiles, largest, (least, zero))
+        top, hit = least, zero
+        for rows in tiles:
+            score = score_a[rows, :]
+            top = jnp.maximum(top, fold(score, jnp.max))
+            hit = hit + fold(jnp.where(ids == pos - rows.start, score, 0.0), jnp.sum)
         top = jnp.max(top, axis=0, keepdims=True)
-
-        def exponentials(t, total):
-            return total + fold(jnp.exp(score_a[tile_of(t), :] - top), jnp.sum)
-
-        total = jnp.sum(lax.fori_loop(0, tiles, exponentials, zero), axis=0, keepdims=True)
+        total = zero
+        for rows in tiles:
+            total = total + fold(jnp.exp(score_a[rows, :] - top), jnp.sum)
+        total = jnp.sum(total, axis=0, keepdims=True)
         za[z, 0:1, half_of(xx)] = top + jnp.log(total)
         za[z, 1:2, half_of(xx)] = jnp.sum(hit, axis=0, keepdims=True)
 
@@ -262,19 +254,18 @@
     arrived(yb.at[others], b_ys, b_yr)
     factor = weight[...] * jnp.exp(tops[...] - lse_of(yb[...]))
 
-    ids = lax.broadcasted_iota(jnp.int32, (TILE, HALF), 0)
-
     def quarter_of(ff, cc):
         return pl.ds(pl.multiple_of((ff * 2 + cc) * QUARTER, QUARTER), QUARTER)
 
     def dscores(ff, cc):
-        rows = quarter_of(ff, cc)
+        start = (ff * 2 + cc) * QUARTER
         for xx in range(NX):
             cols = slice(xx * HALF, (xx + 1) * HALF)
-            match = jnp.where(
-                ids == pos_b[:, cols] - (ff * 2 + cc) * QUARTER, weight[:, cols], 0.0
-            )
-            dsc[rows, cols] = (probs[xx, rows, :] * factor[:, cols] - match).astype(BF16)
+            pos, scale, ratio = pos_b[:, cols] - start, weight[:, cols], factor[:, cols]
+            for r in range(0, QUARTER, TILE):
+                rows = pl.ds(pl.multiple_of(start + r, TILE), TILE)
+                match = jnp.where(ids == pos - r, scale, 0.0)
+                dsc[rows, cols] = (probs[xx, rows, :] * ratio - match).astype(BF16)
 
     def far_copy():
         return remote(gi_s, gi_far, far_s, far_r, other_far)

time: 53.2 us -> 51.3 us (0.964)
  Pallas kernels: 51.9 us -> 50.2 us
    pallas_call x1, Pallas kernels: 51.1 us -> 49.4 us  [per_device(): pl.pallas_call(kernel, out_shape=[pltpu.VMEM(r.shape, r.dtype) for r in r...]
where the time goes in v2:
time: 51.3 us; the launch traced here: 50.8 us
  Pallas kernels  50.2 us (98%)
  between operations  0.64 us (1%)
    pallas_call x1, Pallas kernels, per_device(): pl.pallas_call(kernel, out_shape=[pltpu.VMEM(r.shape, r.dtype) for r in r...  49.4 us

profile of v2, /device:TPU:2, one launch (start us, length us, event | category | flops | bytes accessed | tf_op | source)
XLA Modules:
  0.0 50.8 jit_solution(15254027665068969315)
XLA Ops:
  0.6 49.4 %shard_map.85 = (f32[1,16]{1,0:T(1,128)S(1)}, f32[16,256]{1,0:T(8,128)S(1)}, f32[512,256]{1,0:T(8,128)S(1)}) custom-call(bf16[16,256]{1,0:T(8,128)(2,1)} %qa_in.1, bf16[16,256]{1,0:T(8,128)(2,1)} %qb_in.1, bf16[2048,256]{1,0:T(8,128)(2,1)} %items_in.1, s32[32,128]{1,0:T(8,128)} %bitcast.4, s32[32,128]{1,0:T(8,128)} %bitcast.5, f32[32,128]{1,0:T(8,128)} %bitcast.6), custom_call_target="tpu_custom_call" | custom-call | tf_op jit(solution)/shard_map/pallas_call | solution.py:385
  50.0 0.8 %shard_map.86 = (f32[1,16]{1,0:T(1,128)}, f32[16,256]{1,0:T(8,128)}, f32[512,256]{1,0:T(8,128)}) custom-call(f32[1,16]{1,0:T(1,128)S(1)} %get-tuple-element.9.refs_0_, f32[16,256]{1,0:T(8,128)S(1)} %get-tuple-element.10.refs_1_, f32[512,256]{1,0:T(8,128)S(1)} %get-tuple-element.11.refs_2_), custom_call_target="tpu_custom_call" | custom-call | tf_op jit(solution)/shard_map/pallas_call | solution.py:448

commit v3 on v2

--- a/solution.py
+++ b/solution.py
@@ -10,7 +10,6 @@
 MESH = pl.DeviceIdType.MESH
 F32 = jnp.float32
 BF16 = jnp.bfloat16
-HIGHEST = lax.Precision.HIGHEST
 
 NZ, NY, NX = 8, 4, 2
 OWN = 16
@@ -32,10 +31,24 @@
     )
 
 
-def group_row(table, selector, row_of):
-    picked = jnp.dot(table, selector, precision=HIGHEST, preferred_element_type=F32)
-    rows = lax.broadcasted_iota(jnp.int32, picked.shape, 0)
-    return jnp.sum(jnp.where(rows == row_of, picked, 0.0), axis=0, keepdims=True)
+def exact_parts(table):
+    if table.dtype == jnp.int32:
+        parts = (table & 63, table & (63 << 6), table & (63 << 12))
+        return [part.astype(F32).astype(BF16) for part in parts]
+    high = table.astype(BF16)
+    rest = table - high.astype(F32)
+    middle = rest.astype(BF16)
+    return [high, middle, (rest - middle.astype(F32)).astype(BF16)]
+
+
+def group_rows(tables, selector, row_of):
+    parts = [part for table in tables for part in exact_parts(table)]
+    picked = jnp.dot(jnp.concatenate(parts, axis=0), selector, preferred_element_type=F32)
+    picked = picked.reshape(len(tables), 3, 32, GROUP)
+    rows = lax.broadcasted_iota(jnp.int32, (32, GROUP), 0) == row_of
+    return [
+        jnp.sum(jnp.where(rows, (p[0] + p[1]) + p[2], 0.0), axis=0, keepdims=True) for p in picked
+    ]
 
 
 def lse_of(parts):
@@ -147,26 +160,27 @@
 
     others = pl.ds(0, NZ - 1)
 
+    loads[0].wait()
+    arrived(qb.at[x, y, others], b1_s, b1_r)
+    gather_b_bulk()
+    loads[1].wait()
+    arrived(qa.at[x, y, others], a1_s, a1_r)
+    gather_a_bulk(x)
+
     lanes = lax.broadcasted_iota(jnp.int32, (1, GROUP), 1)
     own_of = lanes % OWN
     z_of = (lanes // OWN) % NZ
     y_of = (lanes // (OWN * NZ)) % NY
     x_of = lanes // (OWN * NZ * NY)
     ks = lax.broadcasted_iota(jnp.int32, (128, GROUP), 0)
-    selector = (ks == x_of * (4 * OWN) + user * OWN + own_of).astype(F32)
-    row_of = z_of * NY + y_of
+    selector = (ks == x_of * (4 * OWN) + user * OWN + own_of).astype(F32).astype(BF16)
     for load in loads[2:5]:
         load.wait()
-    pos_a[...] = group_row(pa_v[...].astype(F32), selector, row_of).astype(jnp.int32) - offset
-    pos_b[...] = group_row(pb_v[...].astype(F32), selector, row_of).astype(jnp.int32) - offset
-    weight[...] = group_row(w_v[...], selector, row_of)
-
-    loads[0].wait()
-    arrived(qb.at[x, y, others], b1_s, b1_r)
-    gather_b_bulk()
-    loads[1].wait()
-    arrived(qa.at[x, y, others], a1_s, a1_r)
-    gather_a_bulk(x)
+    row_a, row_b, weight[...] = group_rows(
+        (pa_v[...], pb_v[...], w_v[...]), selector, z_of * NY + y_of
+    )
+    pos_a[...] = row_a.astype(jnp.int32) - offset
+    pos_b[...] = row_b.astype(jnp.int32) - offset
 
     loads[5].wait()
     for part in range(items_rows // QUARTER):
@@ -347,10 +361,9 @@
     y_parts = ya[...]
     tops[...] = lse_of(y_parts[:, 0:1]) - jnp.sum(y_parts[:, 1:2], axis=0)
     mine = tops[:, pl.ds(pl.multiple_of((x * NY + y) * NZ * OWN, NZ * OWN), NZ * OWN)]
-    pick_row = lax.broadcasted_iota(jnp.int32, (NZ * OWN, OWN), 0)
-    pick_col = lax.broadcasted_iota(jnp.int32, (NZ * OWN, OWN), 1)
-    pick = (pick_row == z * OWN + pick_col).astype(F32)
-    loss_out[...] = jnp.dot(mine, pick, precision=HIGHEST, preferred_element_type=F32)
+    loss_out[...] = pltpu.roll(
+        jnp.broadcast_to(mine, (8, NZ * OWN)), (NZ - z) * OWN % (NZ * OWN), 1
+    )[0:1, 0:OWN]
 
     arrived(r2.at[others], s2s, s2r)
     gq_out[...] = gq_h[z] + jnp.sum(r2[...], axis=0)

time: 51.3 us -> 51.3 us (level)
  no operation moved by 1% of the time
where the time goes in v3:
time: 51.3 us; the launch traced here: 50.9 us
  Pallas kernels  50.2 us (98%)
  between operations  0.64 us (1%)
    pallas_call x1, Pallas kernels, per_device(): pl.pallas_call(kernel, out_shape=[pltpu.VMEM(r.shape, r.dtype) for r in r...  49.4 us

profile of v3, /device:TPU:2, one launch (start us, length us, event | category | flops | bytes accessed | tf_op | source)
XLA Modules:
  0.0 50.9 jit_solution(5747976883292034657)
XLA Ops:
  0.6 49.4 %shard_map.85 = (f32[1,16]{1,0:T(1,128)S(1)}, f32[16,256]{1,0:T(8,128)S(1)}, f32[512,256]{1,0:T(8,128)S(1)}) custom-call(bf16[16,256]{1,0:T(8,128)(2,1)} %qa_in.1, bf16[16,256]{1,0:T(8,128)(2,1)} %qb_in.1, bf16[2048,256]{1,0:T(8,128)(2,1)} %items_in.1, s32[32,128]{1,0:T(8,128)} %bitcast.4, s32[32,128]{1,0:T(8,128)} %bitcast.5, f32[32,128]{1,0:T(8,128)} %bitcast.6), custom_call_target="tpu_custom_call" | custom-call | tf_op jit(solution)/shard_map/pallas_call | solution.py:398
  50.0 0.8 %shard_map.86 = (f32[1,16]{1,0:T(1,128)}, f32[16,256]{1,0:T(8,128)}, f32[512,256]{1,0:T(8,128)}) custom-call(f32[1,16]{1,0:T(1,128)S(1)} %get-tuple-element.9.refs_0_, f32[16,256]{1,0:T(8,128)S(1)} %get-tuple-element.10.refs_1_, f32[512,256]{1,0:T(8,128)S(1)} %get-tuple-element.11.refs_2_), custom_call_target="tpu_custom_call" | custom-call | tf_op jit(solution)/shard_map/pallas_call | solution.py:461

commit v4 on v3

--- a/solution.py
+++ b/solution.py
@@ -266,20 +266,18 @@
     sent(zb.at[others], b_zs, b_zr)
 
     arrived(yb.at[others], b_ys, b_yr)
-    factor = weight[...] * jnp.exp(tops[...] - lse_of(yb[...]))
+    lse_b = lse_of(yb[...])
+    tops[...] = weight[...] * jnp.exp(tops[...] - lse_b)
 
     def quarter_of(ff, cc):
         return pl.ds(pl.multiple_of((ff * 2 + cc) * QUARTER, QUARTER), QUARTER)
 
-    def dscores(ff, cc):
-        start = (ff * 2 + cc) * QUARTER
-        for xx in range(NX):
-            cols = slice(xx * HALF, (xx + 1) * HALF)
-            pos, scale, ratio = pos_b[:, cols] - start, weight[:, cols], factor[:, cols]
-            for r in range(0, QUARTER, TILE):
-                rows = pl.ds(pl.multiple_of(start + r, TILE), TILE)
-                match = jnp.where(ids == pos - r, scale, 0.0)
-                dsc[rows, cols] = (probs[xx, rows, :] * ratio - match).astype(BF16)
+    def dscores(xx):
+        cols = half_of(xx)
+        pos, scale, ratio = pos_b[:, cols], weight[:, cols], tops[:, cols]
+        for rows in tiles:
+            match = jnp.where(ids == pos - rows.start, scale, 0.0)
+            dsc[rows, cols] = (probs[xx, rows, :] * ratio - match).astype(BF16)
 
     def far_copy():
         return remote(gi_s, gi_far, far_s, far_r, other_far)
@@ -308,19 +306,17 @@
         def _():
             remote(gq_s.at[xx, y], r1.at[place], s1s, s1r, at(z, y, xx)).start()
 
-    dscores(1 - far, 1 - core)
+    dscores(1 - x)
+    query_grads(1 - x)
+    dscores(x)
     item_grads(0, 1 - far, 1 - core)
     core_copy(0).start()
-    dscores(1 - far, core)
     item_grads(0, 1 - far, core)
-    dscores(far, 1 - core)
-    dscores(far, core)
-    query_grads(1 - x)
+    query_grads(x)
     core_copy(0).wait_recv()
     gi_s[...] = (gi_f[0, core] + gi_core[0]).astype(BF16)
     far_copy().start()
 
-    query_grads(x)
     item_grads(1, far, 1 - core)
     core_copy(1).start()
     item_grads(1, far, core)

time: 51.3 us -> 51.3 us (level)
  no operation moved by 1% of the time
where the time goes in v4:
time: 51.3 us; the launch traced here: 50.8 us
  Pallas kernels  50.2 us (98%)
  between operations  0.64 us (1%)
    pallas_call x1, Pallas kernels, per_device(): pl.pallas_call(kernel, out_shape=[pltpu.VMEM(r.shape, r.dtype) for r in r...  49.4 us

profile of v4, /device:TPU:2, one launch (start us, length us, event | category | flops | bytes accessed | tf_op | source)
XLA Modules:
  0.0 50.8 jit_solution(12783261775056113991)
XLA Ops:
  0.6 49.4 %shard_map.85 = (f32[1,16]{1,0:T(1,128)S(1)}, f32[16,256]{1,0:T(8,128)S(1)}, f32[512,256]{1,0:T(8,128)S(1)}) custom-call(bf16[16,256]{1,0:T(8,128)(2,1)} %qa_in.1, bf16[16,256]{1,0:T(8,128)(2,1)} %qb_in.1, bf16[2048,256]{1,0:T(8,128)(2,1)} %items_in.1, s32[32,128]{1,0:T(8,128)} %bitcast.4, s32[32,128]{1,0:T(8,128)} %bitcast.5, f32[32,128]{1,0:T(8,128)} %bitcast.6), custom_call_target="tpu_custom_call" | custom-call | tf_op jit(solution)/shard_map/pallas_call | solution.py:394
  50.0 0.8 %shard_map.86 = (f32[1,16]{1,0:T(1,128)}, f32[16,256]{1,0:T(8,128)}, f32[512,256]{1,0:T(8,128)}) custom-call(f32[1,16]{1,0:T(1,128)S(1)} %get-tuple-element.9.refs_0_, f32[16,256]{1,0:T(8,128)S(1)} %get-tuple-element.10.refs_1_, f32[512,256]{1,0:T(8,128)S(1)} %get-tuple-element.11.refs_2_), custom_call_target="tpu_custom_call" | custom-call | tf_op jit(solution)/shard_map/pallas_call | solution.py:457

commit v5 on v4

--- a/solution.py
+++ b/solution.py
@@ -64,7 +64,7 @@
     r1, gq_h, r2,
     gi_f, gi_s, gi_core, gi_far,
     zb, yb, za, ya,
-    tops,
+    tops, top_a,
     in_sem, b1_s, b1_r, b2_s, b2_r, a1_s, a1_r, a2_s, a2_r,
     b_zs, b_zr, b_ys, b_yr, a_zs, a_zr, a_ys, a_yr,
     s1s, s1r, s2s, s2r, gi_ss, gi_rs, far_s, far_r,
@@ -108,7 +108,6 @@
     @pl.loop(1, NZ)
     def _(k):
         pl.semaphore_signal(barrier, inc=1, device_id=at(z_peer(k), y, x), device_id_type=MESH)
-        pl.semaphore_signal(barrier, inc=1, device_id=at(z_peer(k), y, 1 - x), device_id_type=MESH)
 
     @pl.loop(1, NY * NX)
     def _(k):
@@ -123,7 +122,7 @@
     for load in loads:
         load.start()
 
-    pl.semaphore_wait(barrier, 2 * (NZ - 1) + (NY * NX - 1) + 2)
+    pl.semaphore_wait(barrier, (NZ - 1) + (NY * NX - 1) + 2)
 
     def sent(refs, send_sem, recv_sem):
         remote(refs, refs, send_sem, recv_sem, other_core).wait_send()
@@ -221,7 +220,7 @@
         tops[:, half_of(xx)] = top
         zb[z, :, half_of(xx)] = top + jnp.log(total)
 
-    def half_a(xx):
+    def tops_a(xx):
         score_a[...] = scores(qa, xx)
         pos = pos_a[:, half_of(xx)]
         top, hit = least, zero
@@ -229,13 +228,15 @@
             score = score_a[rows, :]
             top = jnp.maximum(top, fold(score, jnp.max))
             hit = hit + fold(jnp.where(ids == pos - rows.start, score, 0.0), jnp.sum)
-        top = jnp.max(top, axis=0, keepdims=True)
-        total = zero
+        top_a[...] = jnp.max(top, axis=0, keepdims=True)
+        za[z, 1:2, half_of(xx)] = jnp.sum(hit, axis=0, keepdims=True)
+
+    def sums_a(xx):
+        top, total = top_a[...], zero
         for rows in tiles:
             total = total + fold(jnp.exp(score_a[rows, :] - top), jnp.sum)
         total = jnp.sum(total, axis=0, keepdims=True)
         za[z, 0:1, half_of(xx)] = top + jnp.log(total)
-        za[z, 1:2, half_of(xx)] = jnp.sum(hit, axis=0, keepdims=True)
 
     def z_round(buf, ss, rs):
         @pl.loop(1, NZ)
@@ -258,11 +259,12 @@
     sent(qa.at[x, y, others], a1_s, a1_r)
     sent(qb.at[0], b2_s, b2_r.at[0])
     sent(qb.at[0, pl.ds(0, NY - 1)], b2_s, b2_r.at[0])
+    arrived(qa.at[x, :, others], a2_s, a2_r.at[x])
+    tops_a(x)
     arrived(zb.at[others], b_zs, b_zr)
     yb[place] = lse_of(zb[...])
     plane_round(yb, b_ys, b_yr)
-    arrived(qa.at[x, :, others], a2_s, a2_r.at[x])
-    half_a(x)
+    sums_a(x)
     sent(zb.at[others], b_zs, b_zr)
 
     arrived(yb.at[others], b_ys, b_yr)
@@ -272,11 +274,13 @@
     def quarter_of(ff, cc):
         return pl.ds(pl.multiple_of((ff * 2 + cc) * QUARTER, QUARTER), QUARTER)
 
-    def dscores(xx):
+    def dscores(xx, ff, cc):
         cols = half_of(xx)
-        pos, scale, ratio = pos_b[:, cols], weight[:, cols], tops[:, cols]
-        for rows in tiles:
-            match = jnp.where(ids == pos - rows.start, scale, 0.0)
+        start = (ff * 2 + cc) * QUARTER
+        pos, scale, ratio = pos_b[:, cols] - start, weight[:, cols], tops[:, cols]
+        for r in range(0, QUARTER, TILE):
+            rows = pl.ds(pl.multiple_of(start + r, TILE), TILE)
+            match = jnp.where(ids == pos - r, scale, 0.0)
             dsc[rows, cols] = (probs[xx, rows, :] * ratio - match).astype(BF16)
 
     def far_copy():
@@ -306,12 +310,16 @@
         def _():
             remote(gq_s.at[xx, y], r1.at[place], s1s, s1r, at(z, y, xx)).start()
 
-    dscores(1 - x)
+    for quarter in range(4):
+        dscores(1 - x, quarter // 2, quarter % 2)
     query_grads(1 - x)
-    dscores(x)
+    dscores(x, 1 - far, 1 - core)
     item_grads(0, 1 - far, 1 - core)
     core_copy(0).start()
+    dscores(x, 1 - far, core)
     item_grads(0, 1 - far, core)
+    dscores(x, far, 1 - core)
+    dscores(x, far, core)
     query_grads(x)
     core_copy(0).wait_recv()
     gi_s[...] = (gi_f[0, core] + gi_core[0]).astype(BF16)
@@ -322,7 +330,8 @@
     item_grads(1, far, core)
 
     arrived(qa.at[1 - x, :, others], a2_s, a2_r.at[1 - x])
-    half_a(1 - x)
+    tops_a(1 - x)
+    sums_a(1 - x)
     z_round(za, a_zs, a_zr)
 
     r1[place] = jnp.zeros((NZ, OWN, E), BF16)
@@ -424,6 +433,7 @@
             pltpu.VMEM((NZ, 2, GROUP), F32),
             pltpu.VMEM((NY * NX, 2, GROUP), F32),
             pltpu.VMEM((1, GROUP), F32),
+            pltpu.VMEM((1, HALF), F32),
             dma((6,)),
             dma, dma,
             dma, dma((NX,)),

time: 51.3 us -> 51.7 us (level)
  no operation moved by 1% of the time
where the time goes in v5:
time: 51.7 us; the launch traced here: 50.7 us
  Pallas kernels  50.1 us (97%)
  between operations  0.64 us (1%)
    pallas_call x1, Pallas kernels, per_device(): pl.pallas_call(kernel, out_shape=[pltpu.VMEM(r.shape, r.dtype) for r in r...  49.2 us

profile of v5, /device:TPU:2, one launch (start us, length us, event | category | flops | bytes accessed | tf_op | source)
XLA Modules:
  0.0 50.7 jit_solution(5672518520864136421)
XLA Ops:
  0.6 49.2 %shard_map.85 = (f32[1,16]{1,0:T(1,128)S(1)}, f32[16,256]{1,0:T(8,128)S(1)}, f32[512,256]{1,0:T(8,128)S(1)}) custom-call(bf16[16,256]{1,0:T(8,128)(2,1)} %qa_in.1, bf16[16,256]{1,0:T(8,128)(2,1)} %qb_in.1, bf16[2048,256]{1,0:T(8,128)(2,1)} %items_in.1, s32[32,128]{1,0:T(8,128)} %bitcast.4, s32[32,128]{1,0:T(8,128)} %bitcast.5, f32[32,128]{1,0:T(8,128)} %bitcast.6), custom_call_target="tpu_custom_call" | custom-call | tf_op jit(solution)/shard_map/pallas_call | solution.py:403
  49.9 0.8 %shard_map.86 = (f32[1,16]{1,0:T(1,128)}, f32[16,256]{1,0:T(8,128)}, f32[512,256]{1,0:T(8,128)}) custom-call(f32[1,16]{1,0:T(1,128)S(1)} %get-tuple-element.9.refs_0_, f32[16,256]{1,0:T(8,128)S(1)} %get-tuple-element.10.refs_1_, f32[512,256]{1,0:T(8,128)S(1)} %get-tuple-element.11.refs_2_), custom_call_target="tpu_custom_call" | custom-call | tf_op jit(solution)/shard_map/pallas_call | solution.py:467

commit v6 on v5

--- a/solution.py
+++ b/solution.py
@@ -61,13 +61,13 @@
     loss_out, gq_out, gi_out,
     items_v, items_t, qa, qb, pa_v, pb_v, w_v, pos_a, pos_b, weight,
     probs, score_a, dsc, gq_f, gq_s,
-    r1, gq_h, r2,
+    r1, rz, gq_h, gq_p, r2, r3,
     gi_f, gi_s, gi_core, gi_far,
     zb, yb, za, ya,
     tops, top_a,
     in_sem, b1_s, b1_r, b2_s, b2_r, a1_s, a1_r, a2_s, a2_r,
     b_zs, b_zr, b_ys, b_yr, a_zs, a_zr, a_ys, a_yr,
-    s1s, s1r, s2s, s2r, gi_ss, gi_rs, far_s, far_r,
+    s1s, s1r, zs, zr, s2s, s2r, s3s, s3r, gi_ss, gi_rs, far_s, far_r,
 ):
     item = lax.axis_index("item")
     user = lax.axis_index("user")
@@ -301,18 +301,32 @@
         gq_f[xx] = block
         gq_s[xx] = block.astype(BF16)
 
+    def plane_send(xx, yy):
+        remote(gq_s.at[xx, yy], r1.at[x, y], s1s, s1r.at[x], at(z, yy, xx)).start()
+
+    def own_sends():
         @pl.loop(1, NY)
         def _(k):
-            yy = y_peer(k)
-            remote(gq_s.at[xx, yy], r1.at[place], s1s, s1r, at(z, yy, xx)).start()
-
-        @pl.when(x != xx)
+            plane_send(x, y_peer(k))
+
+    def other_sends():
+        @pl.when(core == 0)
         def _():
-            remote(gq_s.at[xx, y], r1.at[place], s1s, s1r, at(z, y, xx)).start()
+            @pl.loop(0, NY)
+            def _(k):
+                plane_send(1 - x, y_peer(k))
+
+        @pl.when(core == 1)
+        def _():
+            @pl.loop(1, NZ)
+            def _(k):
+                zz = z_peer(k)
+                remote(gq_s.at[1 - x, :, zz], rz.at[z], zs, zr, at(zz, y, x)).start()
 
     for quarter in range(4):
         dscores(1 - x, quarter // 2, quarter % 2)
     query_grads(1 - x)
+    other_sends()
     dscores(x, 1 - far, 1 - core)
     item_grads(0, 1 - far, 1 - core)
     core_copy(0).start()
@@ -321,6 +335,7 @@
     dscores(x, far, 1 - core)
     dscores(x, far, core)
     query_grads(x)
+    own_sends()
     core_copy(0).wait_recv()
     gi_s[...] = (gi_f[0, core] + gi_core[0]).astype(BF16)
     far_copy().start()
@@ -334,15 +349,31 @@
     sums_a(1 - x)
     z_round(za, a_zs, a_zr)
 
-    r1[place] = jnp.zeros((NZ, OWN, E), BF16)
+    r1[x, y] = jnp.zeros((NZ, OWN, E), BF16)
+    rz[z] = jnp.zeros((NY, OWN, E), BF16)
     r2[z] = jnp.zeros((OWN, E), F32)
-    arrived(r1.at[others], s1s, s1r)
-    gq_h[...] = gq_f[x, y] + jnp.sum(r1[...].astype(F32), axis=0)
+    arrived(r1.at[x, pl.ds(0, NY - 1)], s1s, s1r.at[x])
+    gq_h[...] = gq_f[x, y] + jnp.sum(r1[x].astype(F32), axis=0)
+
+    @pl.when(core == 0)
+    def _():
+        arrived(r1.at[1 - x], s1s, s1r.at[1 - x])
+        gq_h[...] += jnp.sum(r1[1 - x].astype(F32), axis=0)
 
     @pl.loop(1, NZ)
     def _(k):
         zz = z_peer(k)
         remote(gq_h.at[zz], r2.at[z], s2s, s2r, at(zz, y, x)).start()
+
+    @pl.when(core == 1)
+    def _():
+        arrived(rz.at[others], zs, zr)
+        gq_p[...] = gq_f[1 - x, :, z] + jnp.sum(rz[...].astype(F32), axis=0)
+
+        @pl.loop(0, NY)
+        def _(k):
+            yy = y_peer(k)
+            remote(gq_p.at[yy], r3.at[y], s3s, s3r, at(z, yy, 1 - x)).start()
 
     arrived(za.at[others], a_zs, a_zr)
     z_parts = za[...]
@@ -356,7 +387,16 @@
     sent(qa.at[1, :, others], a2_s, a2_r.at[0])
     sent(yb.at[others], b_ys, b_yr)
     sent(za.at[others], a_zs, a_zr)
-    sent(r1.at[others], s1s, s1r)
+    sent(r1.at[0, pl.ds(0, NY - 1)], s1s, s1r.at[0])
+
+    @pl.when(core == 0)
+    def _():
+        sent(r1.at[0], s1s, s1r.at[0])
+
+    @pl.when(core == 1)
+    def _():
+        sent(rz.at[others], zs, zr)
+
     core_copy(0).wait_send()
     core_copy(1).wait_send()
     far_copy().wait_recv()
@@ -372,6 +412,13 @@
 
     arrived(r2.at[others], s2s, s2r)
     gq_out[...] = gq_h[z] + jnp.sum(r2[...], axis=0)
+
+    @pl.when(core == 1)
+    def _():
+        arrived(r3, s3s, s3r)
+        gq_out[...] += jnp.sum(r3[...], axis=0)
+        sent(r3, s3s, s3r)
+
 
     sent(ya.at[others], a_ys, a_yr)
     sent(r2.at[others], s2s, s2r)
@@ -421,9 +468,12 @@
             pltpu.VMEM((rows, GROUP), BF16),
             pltpu.VMEM(block, F32),
             pltpu.VMEM(block, BF16),
-            pltpu.VMEM((NY * NX, NZ, OWN, E), BF16),
+            pltpu.VMEM(block, BF16),
+            pltpu.VMEM((NZ, NY, OWN, E), BF16),
             pltpu.VMEM((NZ, OWN, E), F32),
+            pltpu.VMEM((NY, OWN, E), F32),
             pltpu.VMEM((NZ, OWN, E), F32),
+            pltpu.VMEM((NY, OWN, E), F32),
             pltpu.VMEM((2, 2, QUARTER, E), F32),
             pltpu.VMEM((QUARTER, E), BF16),
             pltpu.VMEM((2, QUARTER, E), F32),
@@ -442,6 +492,8 @@
             dma, dma,
             dma, dma,
             dma, dma,
+            dma, dma,
+            dma, dma((NX,)),
             dma, dma,
             dma, dma,
             dma, dma,

time: 51.7 us -> 51 us (0.986); the launches traced: 50.7 us -> 50.8 us
  no operation moved by 1% of the time
where the time goes in v6:
time: 51 us; the launch traced here: 50.8 us
  Pallas kernels  50.2 us (98%)
  between operations  0.64 us (1%)
    pallas_call x1, Pallas kernels, per_device(): pl.pallas_call(kernel, out_shape=[pltpu.VMEM(r.shape, r.dtype) for r in r...  49.3 us

profile of v6, /device:TPU:2, one launch (start us, length us, event | category | flops | bytes accessed | tf_op | source)
XLA Modules:
  0.0 50.8 jit_solution(12101044586083715764)
XLA Ops:
  0.6 49.3 %shard_map.85 = (f32[1,16]{1,0:T(1,128)S(1)}, f32[16,256]{1,0:T(8,128)S(1)}, f32[512,256]{1,0:T(8,128)S(1)}) custom-call(bf16[16,256]{1,0:T(8,128)(2,1)} %qa_in.1, bf16[16,256]{1,0:T(8,128)(2,1)} %qb_in.1, bf16[2048,256]{1,0:T(8,128)(2,1)} %items_in.1, s32[32,128]{1,0:T(8,128)} %bitcast.4, s32[32,128]{1,0:T(8,128)} %bitcast.5, f32[32,128]{1,0:T(8,128)} %bitcast.6), custom_call_target="tpu_custom_call" | custom-call | tf_op jit(solution)/shard_map/pallas_call | solution.py:450
  50.0 0.8 %shard_map.86 = (f32[1,16]{1,0:T(1,128)}, f32[16,256]{1,0:T(8,128)}, f32[512,256]{1,0:T(8,128)}) custom-call(f32[1,16]{1,0:T(1,128)S(1)} %get-tuple-element.9.refs_0_, f32[16,256]{1,0:T(8,128)S(1)} %get-tuple-element.10.refs_1_, f32[512,256]{1,0:T(8,128)S(1)} %get-tuple-element.11.refs_2_), custom_call_target="tpu_custom_call" | custom-call | tf_op jit(solution)/shard_map/pallas_call | solution.py:519

commit v7 on v6

--- a/solution.py
+++ b/solution.py
@@ -130,41 +130,83 @@
     def arrived(refs, send_sem, recv_sem):
         remote(refs, refs, send_sem, recv_sem, other_core).wait_recv()
 
-    @pl.loop(1, NZ)
-    def _(k):
-        remote(qb_in, qb.at[x, y, z], b1_s, b1_r, at(z_peer(k), y, x)).start()
-
-    def gather_b_bulk():
-        block = qb.at[x, y]
+    others = pl.ds(0, NZ - 1)
+
+    def on_core(number):
+        return pl.when(core == number)
+
+    def small_z(source, q, ss, rs):
+        @pl.loop(1, NZ)
+        def _(k):
+            remote(source, q.at[x, y, z], ss, rs, at(z_peer(k), y, x)).start()
+
+    def small_plane(source, q, ss, rs):
+        @pl.loop(1, NY * NX)
+        def _(k):
+            p = plane_peer(k)
+            remote(source, q.at[x, y, z], ss, rs, at(z, p // NX, p % NX)).start()
+
+    def bulk_plane(q, ss, rs):
+        block = q.at[x, y]
 
         @pl.loop(1, NY)
         def _(k):
-            remote(block, block, b2_s, b2_r.at[x], at(z, y_peer(k), x)).start()
+            remote(block, block, ss, rs.at[x], at(z, y_peer(k), x)).start()
 
         @pl.loop(0, NY)
         def _(k):
-            remote(block, block, b2_s, b2_r.at[x], at(z, y_peer(k), 1 - x)).start()
-
-    @pl.loop(1, NY * NX)
-    def _(k):
-        p = plane_peer(k)
-        remote(qa_in, qa.at[x, y, z], a1_s, a1_r, at(z, p // NX, p % NX)).start()
-
-    def gather_a_bulk(xx):
-        block = qa.at[xx, :, z]
+            remote(block, block, ss, rs.at[x], at(z, y_peer(k), 1 - x)).start()
+
+    def bulk_z(q, ss, rs, xx):
+        block = q.at[xx, :, z]
 
         @pl.loop(1, NZ)
         def _(k):
-            remote(block, block, a2_s, a2_r.at[xx], at(z_peer(k), y, x)).start()
-
-    others = pl.ds(0, NZ - 1)
+            remote(block, block, ss, rs.at[xx], at(z_peer(k), y, x)).start()
+
+    def plane_own_wait(q, ss, rs):
+        arrived(q.at[x, pl.ds(0, NY - 1)], ss, rs.at[x])
+
+    def plane_other_wait(q, ss, rs):
+        arrived(q.at[1 - x], ss, rs.at[1 - x])
+
+    def z_wait(q, ss, rs, xx):
+        arrived(q.at[xx, :, others], ss, rs.at[xx])
+
+    def plane_drain(q, ss, rs):
+        sent(q.at[0], ss, rs.at[0])
+        sent(q.at[0, pl.ds(0, NY - 1)], ss, rs.at[0])
+
+    def z_drain(q, ss, rs):
+        sent(q.at[0, :, others], ss, rs.at[0])
+        sent(q.at[1, :, others], ss, rs.at[0])
+
+    bulk_b, bulk_a = (qb, b2_s, b2_r), (qa, a2_s, a2_r)
+
+    @on_core(0)
+    def _():
+        small_z(qb_in, qb, b1_s, b1_r)
+        small_plane(qa_in, qa, a1_s, a1_r)
+
+    @on_core(1)
+    def _():
+        small_plane(qb_in, qb, b1_s, b1_r)
+        small_z(qa_in, qa, a1_s, a1_r)
 
     loads[0].wait()
     arrived(qb.at[x, y, others], b1_s, b1_r)
-    gather_b_bulk()
+
+    @on_core(0)
+    def _():
+        bulk_plane(*bulk_b)
+
+    @on_core(1)
+    def _():
+        bulk_z(*bulk_b, x)
+        bulk_z(*bulk_b, 1 - x)
+
     loads[1].wait()
     arrived(qa.at[x, y, others], a1_s, a1_r)
-    gather_a_bulk(x)
 
     lanes = lax.broadcasted_iota(jnp.int32, (1, GROUP), 1)
     own_of = lanes % OWN
@@ -249,17 +291,42 @@
             p = plane_peer(k)
             remote(buf.at[place], buf.at[place], ss, rs, at(z, p // NX, p % NX)).start()
 
-    arrived(qb.at[x, pl.ds(0, NY - 1)], b2_s, b2_r.at[x])
+    @on_core(0)
+    def _():
+        plane_own_wait(*bulk_b)
+        bulk_z(*bulk_a, x)
+
+    @on_core(1)
+    def _():
+        z_wait(*bulk_b, x)
+
     half_b(x)
-    arrived(qb.at[1 - x], b2_s, b2_r.at[1 - x])
+
+    @on_core(0)
+    def _():
+        plane_other_wait(*bulk_b)
+
+    @on_core(1)
+    def _():
+        z_wait(*bulk_b, 1 - x)
+        bulk_plane(*bulk_a)
+
     half_b(1 - x)
     z_round(zb, b_zs, b_zr)
-    gather_a_bulk(1 - x)
     sent(qb.at[x, y, others], b1_s, b1_r)
     sent(qa.at[x, y, others], a1_s, a1_r)
-    sent(qb.at[0], b2_s, b2_r.at[0])
-    sent(qb.at[0, pl.ds(0, NY - 1)], b2_s, b2_r.at[0])
-    arrived(qa.at[x, :, others], a2_s, a2_r.at[x])
+
+    @on_core(0)
+    def _():
+        bulk_z(*bulk_a, 1 - x)
+        plane_drain(*bulk_b)
+        z_wait(*bulk_a, x)
+
+    @on_core(1)
+    def _():
+        z_drain(*bulk_b)
+        plane_own_wait(*bulk_a)
+
     tops_a(x)
     arrived(zb.at[others], b_zs, b_zr)
     yb[place] = lse_of(zb[...])
@@ -344,7 +411,14 @@
     core_copy(1).start()
     item_grads(1, far, core)
 
-    arrived(qa.at[1 - x, :, others], a2_s, a2_r.at[1 - x])
+    @on_core(0)
+    def _():
+        z_wait(*bulk_a, 1 - x)
+
+    @on_core(1)
+    def _():
+        plane_other_wait(*bulk_a)
+
     tops_a(1 - x)
     sums_a(1 - x)
     z_round(za, a_zs, a_zr)
@@ -383,8 +457,15 @@
 
     core_copy(1).wait_recv()
     gi_out[...] = gi_f[1, core] + gi_core[1]
-    sent(qa.at[0, :, others], a2_s, a2_r.at[0])
-    sent(qa.at[1, :, others], a2_s, a2_r.at[0])
+
+    @on_core(0)
+    def _():
+        z_drain(*bulk_a)
+
+    @on_core(1)
+    def _():
+        plane_drain(*bulk_a)
+
     sent(yb.at[others], b_ys, b_yr)
     sent(za.at[others], a_zs, a_zr)
     sent(r1.at[0, pl.ds(0, NY - 1)], s1s, s1r.at[0])

time: 51 us -> 51.1 us (level); the launches traced: 50.8 us -> 50.2 us
  Pallas kernels: 50.2 us -> 49.6 us
    pallas_call x1, Pallas kernels: 49.3 us -> 48.7 us  [per_device(): pl.pallas_call(kernel, out_shape=[pltpu.VMEM(r.shape, r.dtype) for r in r...]
where the time goes in v7:
time: 51.1 us; the launch traced here: 50.2 us
  Pallas kernels  49.6 us (97%)
  between operations  0.64 us (1%)
    pallas_call x1, Pallas kernels, per_device(): pl.pallas_call(kernel, out_shape=[pltpu.VMEM(r.shape, r.dtype) for r in r...  48.7 us

profile of v7, /device:TPU:2, one launch (start us, length us, event | category | flops | bytes accessed | tf_op | source)
XLA Modules:
  0.0 50.2 jit_solution(17214244918568258758)
XLA Ops:
  0.6 48.7 %shard_map.85 = (f32[1,16]{1,0:T(1,128)S(1)}, f32[16,256]{1,0:T(8,128)S(1)}, f32[512,256]{1,0:T(8,128)S(1)}) custom-call(bf16[16,256]{1,0:T(8,128)(2,1)} %qa_in.1, bf16[16,256]{1,0:T(8,128)(2,1)} %qb_in.1, bf16[2048,256]{1,0:T(8,128)(2,1)} %items_in.1, s32[32,128]{1,0:T(8,128)} %bitcast.4, s32[32,128]{1,0:T(8,128)} %bitcast.5, f32[32,128]{1,0:T(8,128)} %bitcast.6), custom_call_target="tpu_custom_call" | custom-call | tf_op jit(solution)/shard_map/pallas_call | solution.py:531
  49.4 0.8 %shard_map.86 = (f32[1,16]{1,0:T(1,128)}, f32[16,256]{1,0:T(8,128)}, f32[512,256]{1,0:T(8,128)}) custom-call(f32[1,16]{1,0:T(1,128)S(1)} %get-tuple-element.9.refs_0_, f32[16,256]{1,0:T(8,128)S(1)} %get-tuple-element.10.refs_1_, f32[512,256]{1,0:T(8,128)S(1)} %get-tuple-element.11.refs_2_), custom_call_target="tpu_custom_call" | custom-call | tf_op jit(solution)/shard_map/pallas_call | solution.py:600

commit v8 on v7

--- a/solution.py
+++ b/solution.py
@@ -390,23 +390,23 @@
                 zz = z_peer(k)
                 remote(gq_s.at[1 - x, :, zz], rz.at[z], zs, zr, at(zz, y, x)).start()
 
-    for quarter in range(4):
-        dscores(1 - x, quarter // 2, quarter % 2)
+    for cc in (1 - core, core):
+        dscores(1 - x, 1 - far, cc)
+        dscores(x, 1 - far, cc)
+        item_grads(0, 1 - far, cc)
+        if cc is not core:
+            core_copy(0).start()
+    dscores(1 - x, far, 0)
+    dscores(1 - x, far, 1)
     query_grads(1 - x)
     other_sends()
-    dscores(x, 1 - far, 1 - core)
-    item_grads(0, 1 - far, 1 - core)
-    core_copy(0).start()
-    dscores(x, 1 - far, core)
-    item_grads(0, 1 - far, core)
-    dscores(x, far, 1 - core)
-    dscores(x, far, core)
-    query_grads(x)
-    own_sends()
     core_copy(0).wait_recv()
     gi_s[...] = (gi_f[0, core] + gi_core[0]).astype(BF16)
     far_copy().start()
-
+    dscores(x, far, 0)
+    dscores(x, far, 1)
+    query_grads(x)
+    own_sends()
     item_grads(1, far, 1 - core)
     core_copy(1).start()
     item_grads(1, far, core)

time: 51.1 us -> 50.9 us (level)
  no operation moved by 1% of the time
where the time goes in v8:
time: 50.9 us; the launch traced here: 50.3 us
  Pallas kernels  49.7 us (98%)
  between operations  0.64 us (1%)
    pallas_call x1, Pallas kernels, per_device(): pl.pallas_call(kernel, out_shape=[pltpu.VMEM(r.shape, r.dtype) for r in r...  48.8 us

profile of v8, /device:TPU:2, one launch (start us, length us, event | category | flops | bytes accessed | tf_op | source)
XLA Modules:
  0.0 50.3 jit_solution(17394925025240389235)
XLA Ops:
  0.6 48.8 %shard_map.85 = (f32[1,16]{1,0:T(1,128)S(1)}, f32[16,256]{1,0:T(8,128)S(1)}, f32[512,256]{1,0:T(8,128)S(1)}) custom-call(bf16[16,256]{1,0:T(8,128)(2,1)} %qa_in.1, bf16[16,256]{1,0:T(8,128)(2,1)} %qb_in.1, bf16[2048,256]{1,0:T(8,128)(2,1)} %items_in.1, s32[32,128]{1,0:T(8,128)} %bitcast.4, s32[32,128]{1,0:T(8,128)} %bitcast.5, f32[32,128]{1,0:T(8,128)} %bitcast.6), custom_call_target="tpu_custom_call" | custom-call | tf_op jit(solution)/shard_map/pallas_call | solution.py:531
  49.5 0.8 %shard_map.86 = (f32[1,16]{1,0:T(1,128)}, f32[16,256]{1,0:T(8,128)}, f32[512,256]{1,0:T(8,128)}) custom-call(f32[1,16]{1,0:T(1,128)S(1)} %get-tuple-element.9.refs_0_, f32[16,256]{1,0:T(8,128)S(1)} %get-tuple-element.10.refs_1_, f32[512,256]{1,0:T(8,128)S(1)} %get-tuple-element.11.refs_2_), custom_call_target="tpu_custom_call" | custom-call | tf_op jit(solution)/shard_map/pallas_call | solution.py:600

commit v9 on v8

--- a/solution.py
+++ b/solution.py
@@ -407,21 +407,22 @@
     dscores(x, far, 1)
     query_grads(x)
     own_sends()
+
+    @on_core(0)
+    def _():
+        z_wait(*bulk_a, 1 - x)
+
+    @on_core(1)
+    def _():
+        plane_other_wait(*bulk_a)
+
+    tops_a(1 - x)
+    sums_a(1 - x)
+    z_round(za, a_zs, a_zr)
+
     item_grads(1, far, 1 - core)
     core_copy(1).start()
     item_grads(1, far, core)
-
-    @on_core(0)
-    def _():
-        z_wait(*bulk_a, 1 - x)
-
-    @on_core(1)
-    def _():
-        plane_other_wait(*bulk_a)
-
-    tops_a(1 - x)
-    sums_a(1 - x)
-    z_round(za, a_zs, a_zr)
 
     r1[x, y] = jnp.zeros((NZ, OWN, E), BF16)
     rz[z] = jnp.zeros((NY, OWN, E), BF16)

time: 50.9 us -> 51 us (level)
  no operation moved by 1% of the time
where the time goes in v9:
time: 51 us; the launch traced here: 50.3 us
  Pallas kernels  49.7 us (97%)
  between operations  0.64 us (1%)
    pallas_call x1, Pallas kernels, per_device(): pl.pallas_call(kernel, out_shape=[pltpu.VMEM(r.shape, r.dtype) for r in r...  48.8 us

profile of v9, /device:TPU:2, one launch (start us, length us, event | category | flops | bytes accessed | tf_op | source)
XLA Modules:
  0.0 50.3 jit_solution(13557156066701681610)
XLA Ops:
  0.6 48.8 %shard_map.85 = (f32[1,16]{1,0:T(1,128)S(1)}, f32[16,256]{1,0:T(8,128)S(1)}, f32[512,256]{1,0:T(8,128)S(1)}) custom-call(bf16[16,256]{1,0:T(8,128)(2,1)} %qa_in.1, bf16[16,256]{1,0:T(8,128)(2,1)} %qb_in.1, bf16[2048,256]{1,0:T(8,128)(2,1)} %items_in.1, s32[32,128]{1,0:T(8,128)} %bitcast.4, s32[32,128]{1,0:T(8,128)} %bitcast.5, f32[32,128]{1,0:T(8,128)} %bitcast.6), custom_call_target="tpu_custom_call" | custom-call | tf_op jit(solution)/shard_map/pallas_call | solution.py:532
  49.5 0.8 %shard_map.86 = (f32[1,16]{1,0:T(1,128)}, f32[16,256]{1,0:T(8,128)}, f32[512,256]{1,0:T(8,128)}) custom-call(f32[1,16]{1,0:T(1,128)S(1)} %get-tuple-element.9.refs_0_, f32[16,256]{1,0:T(8,128)S(1)} %get-tuple-element.10.refs_1_, f32[512,256]{1,0:T(8,128)S(1)} %get-tuple-element.11.refs_2_), custom_call_target="tpu_custom_call" | custom-call | tf_op jit(solution)/shard_map/pallas_call | solution.py:601

commit v10 on v9

--- a/solution.py
+++ b/solution.py
@@ -16,7 +16,7 @@
 E = 256
 GROUP = NZ * NY * NX * OWN
 HALF = GROUP // NX
-TILE = 32
+TILE = 16
 QUARTER = 512
 
 

time: 51 us -> 51 us (level)
  no operation moved by 1% of the time
where the time goes in v10:
time: 51 us; the launch traced here: 50.3 us
  Pallas kernels  49.7 us (97%)
  between operations  0.64 us (1%)
    pallas_call x1, Pallas kernels, per_device(): pl.pallas_call(kernel, out_shape=[pltpu.VMEM(r.shape, r.dtype) for r in r...  48.8 us

profile of v10, /device:TPU:2, one launch (start us, length us, event | category | flops | bytes accessed | tf_op | source)
XLA Modules:
  0.0 50.3 jit_solution(10348824474881851064)
XLA Ops:
  0.6 48.8 %shard_map.85 = (f32[1,16]{1,0:T(1,128)S(1)}, f32[16,256]{1,0:T(8,128)S(1)}, f32[512,256]{1,0:T(8,128)S(1)}) custom-call(bf16[16,256]{1,0:T(8,128)(2,1)} %qa_in.1, bf16[16,256]{1,0:T(8,128)(2,1)} %qb_in.1, bf16[2048,256]{1,0:T(8,128)(2,1)} %items_in.1, s32[32,128]{1,0:T(8,128)} %bitcast.4, s32[32,128]{1,0:T(8,128)} %bitcast.5, f32[32,128]{1,0:T(8,128)} %bitcast.6), custom_call_target="tpu_custom_call" | custom-call | tf_op jit(solution)/shard_map/pallas_call | solution.py:532
  49.5 0.8 %shard_map.86 = (f32[1,16]{1,0:T(1,128)}, f32[16,256]{1,0:T(8,128)}, f32[512,256]{1,0:T(8,128)}) custom-call(f32[1,16]{1,0:T(1,128)S(1)} %get-tuple-element.9.refs_0_, f32[16,256]{1,0:T(8,128)S(1)} %get-tuple-element.10.refs_1_, f32[512,256]{1,0:T(8,128)S(1)} %get-tuple-element.11.refs_2_), custom_call_target="tpu_custom_call" | custom-call | tf_op jit(solution)/shard_map/pallas_call | solution.py:601
